TPU v7x, 128 devices: a whole 4x4x4 slice. The times are simulated.
128 devices in a mesh: prompt: 8 (over z, core), seq: 16 (over x, y).
Axes of the slice: x: 4, y: 4, z: 4, core: 2. Of those that a mesh axis runs over, the one named last changes fastest.
Arguments:
- tokens: bfloat16 [8, 2048, 2048], P('prompt', 'seq'), may hold values from -6 to 6
- span_lengths: int32 [8], P('prompt'), may hold values from 512 to 2048, as said below
- state_slots: int32 [8], P('prompt'), may hold values from 0 to 7
- expert_ids: int32 [8, 2048, 10], P('prompt', 'seq'), may hold values from 0 to 255, all different within a row; in each aligned block of 128 rows (0 to 127, 128 to 255, ..., all dimensions but the last counted through in order) at most 8 rows name the same one
- state_pool: float32 [8, 32, 128, 128], P(None, 'seq'), may hold values from -3 to 3
- attn_gain: float32 [2048], replicated, may hold values from 0.5 to 1.5
- w_query: bfloat16 [2048, 2048], P(None, 'seq'), may hold values from -0.125 to 0.125
- w_key: bfloat16 [2048, 2048], P(None, 'seq'), may hold values from -0.125 to 0.125
- w_value: bfloat16 [2048, 4096], P(None, 'seq'), may hold values from -0.125 to 0.125
- w_zgate: bfloat16 [2048, 4096], P(None, 'seq'), may hold values from -0.125 to 0.125
- w_heads: bfloat16 [2048, 2, 32], P(None, None, 'seq'), may hold values from -0.125 to 0.125
- decay_rate: float32 [32], P('seq'), may hold values from 0.00048828125 to 0.1
- head_gain: float32 [128], replicated, may hold values from 0.25 to 2.5
- w_output: bfloat16 [4096, 2048], P('seq'), may hold values from -0.09375 to 0.09375
- moe_gain: float32 [2048], replicated, may hold values from 0.5 to 1.5
- router: bfloat16 [2048, 256], replicated
- w_expert_in: bfloat16 [256, 2048, 1024], P(('prompt', 'seq')), may hold values from -0.125 to 0.125
- w_expert_out: bfloat16 [256, 512, 2048], P(('prompt', 'seq')), may hold values from -0.25 to 0.25
Outputs:
- attended: bfloat16 [8, 2048, 2048], P('prompt', 'seq')
- expert_out: bfloat16 [8, 2048, 2048], P('prompt', 'seq')
- new_states: float32 [8, 32, 128, 128], P('prompt', 'seq')
Inputs may be any that keep to these rules, and one draw needn't show every extreme that they name: `span_lengths`: each prompt's live tokens are its first slots; at least one prompt fills all 2048 slots. `expert_ids`: among the rows of one device no expert is named by more than 8 rows; padded slots are routed too.
All inputs are finite; a program needn't handle non-finite values.
Results may differ from a plain program's by a relative error of at most 0.03.
Values may be sent and summed in bfloat16 or wider, within the bound.
A program may use at most 128 MiB of HBM per device.

v0:
```python
import jax
import jax.numpy as jnp
from jax import lax
from jax.sharding import PartitionSpec as P

DH = 128
CAP = 8
BLK = 256


EPS = 1e-06


def rms_scale(values, gain):
    mean = jnp.mean(values * values, axis=-1, keepdims=True)
    return values * lax.rsqrt(mean + EPS) * gain


def unit_rows(values):
    return values * lax.rsqrt(jnp.sum(values * values, axis=-1, keepdims=True) + EPS)


def block_prepare(query, keys, values, beta, logdec, size):
    span, heads, width = query.shape
    count = span // size

    def blocks(array):
        return jnp.swapaxes(array.reshape((count, size, heads) + array.shape[2:]), 1, 2)

    query, keys, values, beta, logdec = (
        blocks(query),
        blocks(keys),
        blocks(values),
        blocks(beta),
        blocks(logdec),
    )
    highest = lax.Precision.HIGHEST
    cumul = jnp.cumsum(logdec, axis=-1)
    diff = cumul[..., :, None] - cumul[..., None, :]
    rows_iota = lax.broadcasted_iota(jnp.int32, (size, size), 0)
    cols_iota = lax.broadcasted_iota(jnp.int32, (size, size), 1)
    decay = jnp.exp(jnp.minimum(diff, 0.0))
    strict = jnp.where(rows_iota > cols_iota, decay, 0.0)
    within = jnp.where(rows_iota >= cols_iota, decay, 0.0)
    key_key = jnp.einsum("nhid,nhjd->nhij", keys, keys, precision=highest)
    query_key = jnp.einsum("nhid,nhjd->nhij", query, keys, precision=highest)
    system = jnp.eye(size, dtype=jnp.float32) + beta[..., None] * key_key * strict
    start = jnp.exp(cumul)
    right = jnp.concatenate([beta[..., None] * values, (beta * start)[..., None] * keys], axis=-1)
    solved = jax.scipy.linalg.solve_triangular(system, right, lower=True, unit_diagonal=True)
    upd_values = solved[..., :width]
    upd_keys = solved[..., width:]
    tail_keys = jnp.exp(cumul[..., -1:] - cumul)[..., None] * keys
    last = jnp.exp(cumul[..., -1])
    return (upd_values, upd_keys, query_key * within, start, tail_keys, last, query)


def block_step(state, block):
    upd_values, upd_keys, attn, start, tail_keys, last, query = block
    highest = lax.Precision.HIGHEST
    corrected = upd_values - jnp.einsum("hik,hvk->hiv", upd_keys, state, precision=highest)
    output = start[..., None] * jnp.einsum("hik,hvk->hiv", query, state, precision=highest)
    output = output + jnp.einsum("hij,hjv->hiv", attn, corrected, precision=highest)
    new_state = last[:, None, None] * state + jnp.einsum(
        "hiv,hik->hvk", corrected, tail_keys, precision=highest
    )
    return (new_state, output)


def unblock(outputs):
    count, heads, size, width = outputs.shape
    return jnp.swapaxes(outputs, 1, 2).reshape(count * size, heads, width)


def shards(
    tokens,
    span_lengths,
    state_slots,
    expert_ids,
    state_pool,
    attn_gain,
    w_query,
    w_key,
    w_value,
    w_zgate,
    w_heads,
    decay_rate,
    head_gain,
    w_output,
    moe_gain,
    router,
    w_expert_in,
    w_expert_out,
):
    n_seq = lax.axis_size("seq")
    n_prompt = lax.axis_size("prompt")
    local_rows = tokens.shape[1]
    width = tokens.shape[2]
    span = local_rows * n_seq
    key_heads = w_query.shape[1] // DH
    value_heads = w_value.shape[1] // DH
    ratio = value_heads // key_heads
    length = span_lengths[0]
    own_rows = tokens[0]
    normed = rms_scale(own_rows.astype(jnp.float32), attn_gain).astype(jnp.bfloat16)
    head_weights = w_heads.reshape(width, 2 * value_heads)
    weights_all = (w_query, w_key, w_value, w_zgate, head_weights)
    piece = lax.all_gather(normed, "seq", axis=0, tiled=True)
    query, keys, values, zgate, head_logits = tuple(
        (jnp.dot(piece, weight, preferred_element_type=jnp.float32) for weight in weights_all)
    )
    query = jnp.repeat(unit_rows(query.reshape(span, key_heads, DH)) * DH ** (-0.5), ratio, axis=1)
    keys = jnp.repeat(unit_rows(keys.reshape(span, key_heads, DH)), ratio, axis=1)
    values = values.reshape(span, value_heads, DH)
    zgate = zgate.reshape(span, value_heads, DH)
    head_logits = head_logits.reshape(span, 2, value_heads)
    positions = lax.broadcasted_iota(jnp.int32, (span,), 0)
    live = (positions < length).astype(jnp.float32)
    beta = jax.nn.sigmoid(head_logits[:, 1, :]) * live[:, None]
    logdec = -decay_rate[None, :] * jax.nn.softplus(head_logits[:, 0, :]) * live[:, None]
    state = lax.dynamic_index_in_dim(state_pool, state_slots[0], 0, keepdims=False)
    prepared = block_prepare(query, keys, values, beta, logdec, BLK)
    final, outputs = lax.scan(block_step, state, prepared)
    heads = unblock(outputs)
    gated = (
        (rms_scale(heads, head_gain) * jax.nn.silu(zgate))
        .astype(jnp.bfloat16)
        .reshape(span, value_heads * DH)
    )
    summed = lax.psum_scatter(
        jnp.dot(gated, w_output, preferred_element_type=jnp.float32).astype(jnp.bfloat16),
        "seq",
        scatter_dimension=0,
        tiled=True,
    ).astype(jnp.float32)
    own_positions = lax.axis_index("seq") * local_rows + lax.broadcasted_iota(
        jnp.int32, (local_rows,), 0
    )
    own_live = (own_positions < length).astype(jnp.float32)
    attended = (summed * own_live[:, None]).astype(jnp.bfloat16)
    residual = own_rows.astype(jnp.float32) + attended.astype(jnp.float32)
    moe_input = rms_scale(residual, moe_gain).astype(jnp.bfloat16)
    logits = jnp.dot(moe_input, router, preferred_element_type=jnp.float32)
    experts_all = router.shape[1]
    chosen_ids = expert_ids[0]
    top_count = chosen_ids.shape[1]
    table = lax.broadcasted_iota(jnp.int32, (1, 1, experts_all), 2)
    match = chosen_ids[:, :, None] == table
    picked = jnp.sum(jnp.where(match, logits[:, None, :], 0.0), axis=-1)
    weights = jax.nn.softmax(picked, axis=-1) * own_live[:, None]
    flat_match = match.reshape(local_rows * top_count, experts_all).astype(jnp.int32)
    running = jnp.cumsum(flat_match, axis=0) - flat_match
    slot_position = jnp.sum(running * flat_match, axis=1)
    target = chosen_ids.reshape(-1) * CAP + slot_position
    sources = jnp.repeat(moe_input, top_count, axis=0)
    outgoing = jnp.zeros((experts_all * CAP, width), jnp.bfloat16).at[target].set(sources)
    owners = n_prompt * n_seq
    local_experts = experts_all // owners
    arrived = lax.all_to_all(
        outgoing.reshape(owners, local_experts, CAP, width),
        ("prompt", "seq"),
        split_axis=0,
        concat_axis=0,
        tiled=True,
    )
    pair = jnp.einsum("necd,edf->necf", arrived, w_expert_in, preferred_element_type=jnp.float32)
    inner_width = w_expert_out.shape[1]
    inner = (jax.nn.silu(pair[..., :inner_width]) * pair[..., inner_width:]).astype(jnp.bfloat16)
    result = jnp.einsum(
        "necf,efd->necd", inner, w_expert_out, preferred_element_type=jnp.float32
    ).astype(jnp.bfloat16)
    returned = lax.all_to_all(result, ("prompt", "seq"), split_axis=0, concat_axis=0, tiled=True)
    back = returned.reshape(experts_all * CAP, width)[target].reshape(local_rows, top_count, width)
    expert_out = jnp.sum(weights[:, :, None] * back.astype(jnp.float32), axis=1).astype(
        jnp.bfloat16
    )
    return (attended[None], expert_out[None], final[None])


def solution(mesh):
    return jax.shard_map(
        shards,
        mesh=mesh,
        in_specs=(
            P("prompt", "seq", None),
            P("prompt"),
            P("prompt"),
            P("prompt", "seq", None),
            P(None, "seq", None, None),
            P(),
            P(None, "seq"),
            P(None, "seq"),
            P(None, "seq"),
            P(None, "seq"),
            P(None, None, "seq"),
            P("seq"),
            P(),
            P("seq", None),
            P(),
            P(),
            P(("prompt", "seq"), None, None),
            P(("prompt", "seq"), None, None),
        ),
        out_specs=(
            P("prompt", "seq", None),
            P("prompt", "seq", None),
            P("prompt", "seq", None, None),
        ),
        check_vma=False,
    )
```

profile of v0, /device:TPU:5, one launch (start us, length us, event | category | flops | bytes accessed | tf_op | source)
XLA Modules:
  0.0 972.7 jit_solution(18265834159951702629)
XLA Ops:
  16.8 66.9 %all-gather.2.cloned.1.call-done = bf16[2048,2048]{1,0:T(8,128)(2,1)} async-done(((bf16[128,2048]{1,0:T(8,128)(2,1)}), bf16[2048,2048]{1,0:T(8,128)(2,1)}) %all-gather.2.cloned.1.call-update) | async-done | bytes 8388624 | tf_op jit(solution)/shard_map/all_gather | solution.py:108
  83.7 5.6 fusion.17
  99.9 5.9 multiply_reduce_fusion.4
  106.8 6.2 select_add_fusion
  113.1 9.3 while.14
  122.4 315.9 %custom-call.4 = f32[8,2,2,128,128]{3,4,2,1,0:T(8,128)} custom-call(f32[8,2,2,128,128]{4,3,2,1,0:T(8,128)} %bitcast.236), custom_call_target="InvertDiagBlocksLowerTriangular" | custom-call | tf_op jit(solution)/shard_map/jit(_solve_triangular)/vmap(vmap())/triangular_solve | solution.py:50
  438.3 7.3 fusion.84
  468.9 5.5 select_multiply_fusion
  475.9 55.0 %while.13 = (s32[]{:T(128)}, f32[2,128,128]{2,1,0:T(8,128)S(1)}, f32[8,2,256,128]{3,2,1,0:T(8,128)S(1)}, f32[8,2]{1,0:T(8,128)S(1)}, f32[8,2,256,128]{3,2,1,0:T(...) while((s32[]{:T(128)}, f32[2,128,128]{2,1,0:T(8,128)S(1)}, ...), condition=%wide.region_6.7_spmd, body=%wide.region_5.6_spmd.sunk | while | flops 503578624 | bytes 3683469 | solution.py:123
  536.0 4.6 mul.281
  540.7 17.3 %convolution_convert_fusion = bf16[2048,2048]{1,0:T(8,128)(2,1)} fusion(bf16[256,2048]{1,0:T(8,128)(2,1)S(1)} %copy-done, f32[256,8,2,128]{3,2,1,0:T(2,128)S(1)} %bitcast.223, f32[256,8,2,128]{3,2,1,0:T(2,128)} %bitcast.224, f32[256]{0:T(256)S(1)} %copy-done.28, bf16[2048,2048]{1,0:T(8,128)(2,1)} %all-gather.2.cloned.1.call-done, bf16[2048,256]{1,0:T(8,128)(2,1)} %param.29), kind=kOutput, calls=%fused_computation.33 | convolution fusion | flops 4303355904 | bytes 23069696 | tf_op jit(solution)/shard_map/dot_general | solution.py:131
  561.4 79.7 %reduce-scatter.2.cloned.1.call-done = bf16[128,2048]{1,0:T(8,128)(2,1)} async-done(((bf16[2048,2048]{1,0:T(8,128)(2,1)}), bf16[128,2048]{1,0:T(8,128)(2,1)}) %reduce-scatter.2.cloned.1.call-update) | async-done | bytes 524304 | tf_op jit(solution)/shard_map/reduce_scatter | solution.py:130
  644.7 4.4 broadcast_in_dim.51
  649.1 9.8 %reshape.356 = bf16[1280,2048]{1,0:T(8,128)(2,1)} reshape(bf16[128,10,2048]{2,1,0:T(8,128)(2,1)} %broadcast_in_dim.51) | data formatting | bytes 10485760 | tf_op jit(solution)/shard_map/reshape | solution.py:155
  658.9 15.6 %scatter_custom_fusion = bf16[2048,2048]{1,0:T(8,128)(2,1)} fusion(s32[1280]{0:T(1024)S(1)} %fusion.73, bf16[1280,2048]{1,0:T(8,128)(2,1)} %reshape.356, bf16[]{:T(256)} %constant.82.clone.1), kind=kCustom, calls=%fused_computation.41 | custom fusion | bytes 8389120 | tf_op jit(solution)/shard_map/scatter | solution.py:156
  674.5 106.5 %all_to_all.10 = bf16[128,2,8,2048]{3,2,1,0:T(8,128)(2,1)S(1)} all-to-all(bf16[128,2,8,2048]{3,2,1,0:T(8,128)(2,1)} %bitcast.215), channel_id=1, replica_groups=mesh['prompt'=8,'seq'=16] {'prompt','seq'}, dimensions={0} | all-to-all | bytes 16777216 | tf_op jit(solution)/shard_map/all_to_all | solution.py:159
  781.0 18.2 %fusion.24 = f32[128,2,8,1024]{3,0,2,1:T(8,128)} fusion(bf16[2,2048,1024]{2,1,0:T(8,128)(2,1)} %param.36, bf16[128,2,8,2048]{3,2,1,0:T(8,128)(2,1)S(1)} %all_to_all.10), kind=kOutput, calls=%fused_computation.46 | convolution fusion | flops 8589934592 | bytes 25165824 | tf_op jit(solution)/shard_map/necd,edf->necf/dot_general | solution.py:166
  799.3 10.3 %convert_bitcast_fusion = bf16[128,2,8,2048]{3,0,2,1:T(8,128)(2,1)} fusion(bf16[2,512,2048]{2,1,0:T(8,128)(2,1)S(1)} %copy-done.24, f32[128,2,8,1024]{3,0,2,1:T(8,128)} %fusion.24), kind=kOutput, calls=%fused_computation.32 | convolution fusion | flops 4305453056 | bytes 20971520 | tf_op jit(solution)/shard_map/necf,efd->necd/dot_general | solution.py:169
  809.6 11.2 %copy.171 = bf16[128,2,8,2048]{3,2,1,0:T(8,128)(2,1)} copy(bf16[128,2,8,2048]{3,0,2,1:T(8,128)(2,1)} %convert_bitcast_fusion) | data formatting | bytes 16777216 | tf_op jit(solution)/shard_map/convert_element_type | solution.py:171
  820.8 6.6 all-to-all-start.1
  828.4 100.9 %all-to-all-done.1 = bf16[128,2,8,2048]{3,2,1,0:T(8,128)(2,1)} async-done(((bf16[128,2,8,2048]{3,2,1,0:T(8,128)(2,1)}), bf16[128,2,8,2048]{3,2,1,0:T(8,128)(2,1)}, u32[]{:S(2)}, u32[]{:S(2)}) %all-to-all-start.1) | async-done | bytes 8388640 | tf_op jit(solution)/shard_map/all_to_all | solution.py:172
  929.3 15.3 %gather_fusion = bf16[1280,2048]{1,0:T(8,128)(2,1)} fusion(bf16[2048,2048]{1,0:T(8,128)(2,1)} %bitcast.39, s32[2048]{0:T(1024)S(1)} %pad_clamp_fusion), kind=kCustom, calls=%fused_computation | custom fusion | bytes 10490880 | tf_op jit(solution)/shard_map/gather | solution.py:173
  944.6 10.3 %reshape.343 = f32[128,10,2048]{2,1,0:T(8,128)} reshape(bf16[1280,2048]{1,0:T(8,128)(2,1)} %gather_fusion) | data formatting | bytes 15728640 | tf_op jit(solution)/shard_map/convert_element_type | solution.py:174
  954.9 10.5 %multiply_reduce_fusion = bf16[128,2048]{1,0:T(8,128)(2,1)} fusion(f32[128,10,2048]{2,1,0:T(8,128)} %reshape.343, f32[128,10]{1,0:T(8,128)S(1)} %copy.164), kind=kLoop, calls=%fused_computation.26 | loop fusion | flops 4980736 | bytes 11015168 | tf_op jit(solution)/shard_map/reduce_sum | solution.py:174
  (209 shorter events, 120.8 us)
Async XLA Ops:
  7.2 533.5 %copy-start = (bf16[256,2048]{1,0:T(8,128)(2,1)S(1)}, bf16[256,2048]{1,0:T(8,128)(2,1)}, u32[]{:S(2)}) copy-start(bf16[256,2048]{1,0:T(8,128)(2,1)} %param.33) | copy-start | bytes 3145732
  7.2 3.5 copy-start.19
  7.2 4.8 copy-start.26
  7.2 8.3 copy-start.27
  7.2 76.5 %all-gather.2.cloned.1.call-start = ((), (), s32[]{:S(2)}) async-start(), calls=%async_computation.3 | async-start | bytes 8912896 | tf_op jit(solution)/shard_map/all_gather | solution.py:108
  10.6 630.4 %reduce-scatter.2.cloned.1.call-start = ((), (), s32[]{:S(2)}) async-start(), calls=%async_computation.4 | async-start | bytes 8912896 | tf_op jit(solution)/shard_map/reduce_scatter | solution.py:130
  13.2 76.8 %copy-start.11 = (f32[8,256]{1,0:T(8,128)}, f32[8,256]{1,0:T(8,128)S(1)}, u32[]{:S(2)}) copy-start(f32[8,256]{1,0:T(8,128)S(1)} %fusion.71) | copy-start | bytes 24580
  97.3 8.9 copy-start.20
  105.9 7.1 copy-start.13
  106.2 6.7 copy-start.4
  106.8 6.2 copy-start.29
  445.6 3.3 copy-start.14
  455.6 8.0 slice-start
  459.0 4.6 slice-start.1
  463.6 3.5 copy-start.23
  530.9 5.1 copy-start.2
  533.0 3.0 copy-start.7
  536.0 4.7 copy-start.28
  559.8 81.3 %copy-start.3 = (bf16[1,128,2048]{2,1,0:T(8,128)(2,1)S(1)}, bf16[1,128,2048]{2,1,0:T(8,128)(2,1)}, u32[]{:S(2)}) copy-start(bf16[1,128,2048]{2,1,0:T(8,128)(2,1)} %param.20) | copy-start | bytes 1572868
  560.6 81.9 %copy-start.22 = (f32[2048]{0:T(1024)S(1)}, f32[2048]{0:T(1024)}, u32[]{:S(2)}) copy-start(f32[2048]{0:T(1024)} %param.34) | copy-start | bytes 24580
  781.0 18.2 %copy-start.24 = (bf16[2,512,2048]{2,1,0:T(8,128)(2,1)S(1)}, bf16[2,512,2048]{2,1,0:T(8,128)(2,1)}, u32[]{:S(2)}) copy-start(bf16[2,512,2048]{2,1,0:T(8,128)(2,1)} %param.37) | copy-start | bytes 12582916
  820.8 6.6 copy-start.9
  820.8 108.5 %all-to-all-start.1 = ((bf16[128,2,8,2048]{3,2,1,0:T(8,128)(2,1)}), bf16[128,2,8,2048]{3,2,1,0:T(8,128)(2,1)}, u32[]{:S(2)}, u32[]{:S(2)}) async-start(bf16[128,2,8,2048]{3,2,1,0:T(8,128)(2,1)} %copy.171), calls=%async_computation.2 | async-start | bytes 16777216 | tf_op jit(solution)/shard_map/all_to_all | solution.py:172
  954.9 10.5 %copy-start.1 = (bf16[256,2048]{1,0:T(8,128)(2,1)S(1)}, bf16[256,2048]{1,0:T(8,128)(2,1)}, u32[]{:S(2)}) copy-start(bf16[256,2048]{1,0:T(8,128)(2,1)} %param.33) | copy-start | bytes 3145732
  (11 other events, 18.2 us)
Sparse Core Ops, SparseCore 0:
  10.8 72.8 all-gather.1
  558.1 82.8 reduce-scatter.1
where the time goes:
time: 978 us; the launch traced here: 973 us
  other arithmetic  353 us (36%)
  waiting for transfers between devices  247 us (25%)
  matrix products  136 us (14%)
  blocking collectives  107 us (11%)
  local copies, waits for them, and re-layouts  106 us (11%)
  between operations  16.4 us (2%)
    another operation x4, other arithmetic, block_prepare(): jax.scipy.linalg.solve_triangular(system, right, lower=True, unit_diagona...  319 us
    all_to_all x1, blocking collectives, shards(): lax.all_to_all(outgoing.reshape(owners, local_experts, CAP, width), ('pro...  107 us
    all_to_all x1, waiting for transfers between devices, shards(): lax.all_to_all(result, ('prompt', 'seq'), split_axis=0, concat_axis=0, ti...  101 us
    reduce_scatter x1, waiting for transfers between devices, shards(): lax.psum_scatter(jnp.dot(gated, w_output, preferred_element_type=jnp.floa...  79.7 us
    all_gather x1, waiting for transfers between devices, shards(): piece = lax.all_gather(normed, 'seq', axis=0, tiled=True)  66.9 us
    dot_general x4, matrix products, shards(): jnp.dot(piece, weight, preferred_element_type=jnp.float32)  22.3 us
  transfers between devices with their start and end apart: 3, of which 3 were waited for; matrix products, arithmetic and copies ran while one was open for 1% of the time, Pallas kernels for 0%

commit v1 on v0

v1 whole, which is shorter than its diff:
```python
import functools
import jax
import jax.numpy as jnp
from jax import lax
from jax.sharding import PartitionSpec as P
from jax.experimental import pallas as pl
from jax.experimental.pallas import tpu as pltpu

EPS = 1e-06
CH = 128
F32 = jnp.float32
BF16 = jnp.bfloat16


def mm(a, b):
    return jnp.dot(a, b, preferred_element_type=F32)


def halves(a):
    high = a.astype(BF16)
    return high, (a - high.astype(F32)).astype(BF16)


def mm3(a, b):
    a_high, a_low = halves(a)
    b_high, b_low = halves(b)
    wide = mm(jnp.concatenate([a_high, a_low], axis=1), jnp.concatenate([b_high, b_high], axis=0))
    return wide + mm(a_high, b_low)


def unit_lower_inverse(lows, rows, cols):
    eye = jnp.where(rows == cols, 1.0, 0.0)
    inverses = [eye - jnp.where(rows // 2 == cols // 2, low, 0.0) for low in lows]
    size = 2
    while size < CH:
        mask = (rows // (2 * size) == cols // (2 * size)) & (rows // size != cols // size)
        inner = [mm3(jnp.where(mask, low, 0.0), inv) for low, inv in zip(lows, inverses)]
        inverses = [inv - mm3(inv, part) for inv, part in zip(inverses, inner)]
        size *= 2
    return inverses


def delta_body(tile, base, length, proj, rate, gain, state):
    rows = lax.broadcasted_iota(jnp.int32, (CH, CH), 0)
    cols = lax.broadcasted_iota(jnp.int32, (CH, CH), 1)
    tri = jnp.where(rows >= cols, 1.0, 0.0)
    chunks = tile // CH
    prep = []
    lows = []
    for c in range(chunks):
        part = proj[c * CH : (c + 1) * CH]
        q, k = part[:, 0:128], part[:, 128:256]
        q = q * (lax.rsqrt(jnp.sum(q * q, axis=-1, keepdims=True) + EPS) * 128 ** (-0.5))
        k = k * lax.rsqrt(jnp.sum(k * k, axis=-1, keepdims=True) + EPS)
        logits = part[:, 768:896]
        live = jnp.where(base + c * CH + rows < length, 1.0, 0.0)
        softplus = jnp.maximum(logits, 0.0) + jnp.log1p(jnp.exp(-jnp.abs(logits)))
        logdec = -rate * softplus * live
        beta2 = live / (1.0 + jnp.exp(-logits))
        cumul = jnp.dot(tri, logdec, preferred_element_type=F32, precision=lax.Precision.HIGHEST)
        cumul_t = cumul.T
        q_b, k_b = q.astype(BF16), k.astype(BF16)
        kt_b = k.T.astype(BF16)
        both = mm(jnp.concatenate([k_b, q_b], axis=0), kt_b)
        kk, qk = both[:CH], both[CH:]
        per_head = []
        for h in range(2):
            g = cumul[:, h : h + 1]
            decay = jnp.exp(jnp.minimum(g - cumul_t[h : h + 1, :], 0.0))
            beta = beta2[:, 2 + h : 3 + h]
            lows.append(jnp.where(rows > cols, beta * kk * decay, 0.0))
            attn = jnp.where(rows >= cols, qk * decay, 0.0).astype(BF16)
            start = jnp.exp(g)
            value = part[:, 256 + 128 * h : 384 + 128 * h]
            right = jnp.concatenate([beta * value, (beta * start) * k], axis=1).astype(BF16)
            last = cumul[CH - 1 : CH, h : h + 1]
            tail = jnp.exp(last - g)
            per_head.append((attn, start, right, tail, jnp.exp(last)))
        prep.append((q_b, kt_b, per_head))
    inverses = unit_lower_inverse(lows, rows, cols)
    solved = []
    for c in range(chunks):
        for h in range(2):
            high, low = halves(inverses[2 * c + h])
            right = prep[c][2][h][2]
            solved.append(mm(jnp.concatenate([high, low], axis=1), jnp.concatenate([right, right], axis=0)))
    gated = []
    state = list(state)
    for c in range(chunks):
        q_b, kt_b, per_head = prep[c]
        outs = []
        for h in range(2):
            attn, start, _, tail, last = per_head[h]
            upd = solved[2 * c + h]
            left = jnp.concatenate([upd[:, 128:].astype(BF16), q_b], axis=0)
            s_high, s_low = halves(state[h])
            got = mm(jnp.concatenate([left, left], axis=1), jnp.concatenate([s_high, s_low], axis=0))
            corrected = upd[:, :128] - got[:CH]
            out = start * got[CH:] + mm(attn, corrected.astype(BF16))
            t_high, t_low = halves(tail * corrected)
            state[h] = last * state[h] + mm(
                jnp.concatenate([kt_b, kt_b], axis=1), jnp.concatenate([t_high, t_low], axis=0)
            )
            z = proj[c * CH : (c + 1) * CH, 512 + 128 * h : 640 + 128 * h]
            scale = lax.rsqrt(jnp.mean(out * out, axis=-1, keepdims=True) + EPS)
            outs.append((out * scale * gain * (z / (1.0 + jnp.exp(-z)))).astype(BF16))
        gated.append(jnp.concatenate(outs, axis=1))
    return state, jnp.concatenate(gated, axis=0)


def delta_kernel(tile, length_ref, piece_ref, w_ref, rate_ref, gain_ref, wo_ref, first_ref, out_ref, final_ref, state_ref):
    step = pl.program_id(0)

    @pl.when(step == 0)
    def _():
        for h in range(2):
            state_ref[h] = first_ref[h].T

    proj = mm(piece_ref[...], w_ref[...])
    state, gated = delta_body(
        tile, step * tile, length_ref[0], proj, rate_ref[...], gain_ref[...], [state_ref[0], state_ref[1]]
    )
    for h in range(2):
        state_ref[h] = state[h]
    out_ref[...] = mm(gated, wo_ref[...]).astype(BF16)

    @pl.when(step == pl.num_programs(0) - 1)
    def _():
        for h in range(2):
            final_ref[h] = state_ref[h].T


def delta(length, piece, weights, rate, gain, w_output, first, tile=256):
    span, width = piece.shape
    total = weights.shape[1]
    const = lambda *shape: pl.BlockSpec(shape, lambda i: (0,) * len(shape))
    return pl.pallas_call(
        functools.partial(delta_kernel, tile),
        grid=(span // tile,),
        in_specs=[
            pl.BlockSpec(memory_space=pltpu.SMEM),
            pl.BlockSpec((tile, width), lambda i: (i, 0)),
            const(width, total),
            const(1, 128),
            const(1, 128),
            const(*w_output.shape),
            const(2, 128, 128),
        ],
        out_specs=[pl.BlockSpec((tile, w_output.shape[1]), lambda i: (i, 0)), const(2, 128, 128)],
        out_shape=[
            jax.ShapeDtypeStruct((span, w_output.shape[1]), BF16),
            jax.ShapeDtypeStruct((2, 128, 128), F32),
        ],
        scratch_shapes=[pltpu.VMEM((2, 128, 128), F32)],
        compiler_params=pltpu.CompilerParams(vmem_limit_bytes=50 * 2**20),
    )(length, piece, weights, rate, gain, w_output, first)


CAP = 8


def rms_scale(values, gain):
    mean = jnp.mean(values * values, axis=-1, keepdims=True)
    return values * lax.rsqrt(mean + EPS) * gain


def routing(chosen_ids, experts):
    tokens = chosen_ids.shape[0]
    table = lax.broadcasted_iota(jnp.int32, (1, 1, experts), 2)
    member = jnp.any(chosen_ids[:, :, None] == table, axis=1)
    rows = lax.broadcasted_iota(jnp.int32, (tokens, tokens), 0)
    cols = lax.broadcasted_iota(jnp.int32, (tokens, tokens), 1)
    earlier = (rows > cols).astype(BF16)
    before = jnp.dot(earlier, member.astype(BF16), preferred_element_type=F32)
    place = jnp.where(member, before, -1.0).T
    slots = lax.broadcasted_iota(jnp.int32, (1, CAP, 1), 1).astype(F32)
    onehot = (place[:, None, :] == slots).reshape(experts * CAP, tokens)
    return onehot, member


def shards(
    tokens,
    span_lengths,
    state_slots,
    expert_ids,
    state_pool,
    attn_gain,
    w_query,
    w_key,
    w_value,
    w_zgate,
    w_heads,
    decay_rate,
    head_gain,
    w_output,
    moe_gain,
    router,
    w_expert_in,
    w_expert_out,
):
    local_rows, width = tokens.shape[1:]
    length = span_lengths[0]
    own_rows = tokens[0]
    normed = rms_scale(own_rows.astype(F32), attn_gain).astype(BF16)
    head_weights = jnp.pad(w_heads.reshape(width, 4), ((0, 0), (0, 124)))
    weights_all = jnp.concatenate([w_query, w_key, w_value, w_zgate, head_weights], axis=1)
    piece = lax.all_gather(normed, "seq", axis=0, tiled=True)
    first = lax.dynamic_index_in_dim(state_pool, state_slots[0], 0, keepdims=False)
    rate = jnp.pad(decay_rate, (0, 126)).reshape(1, 128)
    partial, final = delta(span_lengths, piece, weights_all, rate, head_gain.reshape(1, 128), w_output, first)
    summed = lax.psum_scatter(partial, "seq", scatter_dimension=0, tiled=True).astype(F32)
    own_positions = lax.axis_index("seq") * local_rows + lax.broadcasted_iota(jnp.int32, (local_rows, 1), 0)
    own_live = (own_positions < length).astype(F32)
    attended = (summed * own_live).astype(BF16)
    residual = own_rows.astype(F32) + attended.astype(F32)
    moe_input = rms_scale(residual, moe_gain).astype(BF16)
    logits = jnp.dot(moe_input, router, preferred_element_type=F32)
    experts_all = router.shape[1]
    onehot, member = routing(expert_ids[0], experts_all)
    top = jnp.max(jnp.where(member, logits, -jnp.inf), axis=-1, keepdims=True)
    powers = jnp.where(member, jnp.exp(logits - top), 0.0)
    weights = powers / jnp.sum(powers, axis=-1, keepdims=True) * own_live
    spread = jnp.broadcast_to(weights.T[:, None, :], (experts_all, CAP, local_rows)).reshape(onehot.shape)
    combine = jnp.where(onehot, spread, 0.0).astype(BF16)
    outgoing = jnp.dot(onehot.astype(BF16), moe_input, preferred_element_type=F32).astype(BF16)
    local_experts = w_expert_in.shape[0]
    owners = experts_all // local_experts
    arrived = lax.all_to_all(
        outgoing.reshape(owners, local_experts, CAP, width),
        ("prompt", "seq"),
        split_axis=0,
        concat_axis=0,
        tiled=True,
    )
    pair = jnp.einsum("necd,edf->necf", arrived, w_expert_in, preferred_element_type=F32)
    inner_width = w_expert_out.shape[1]
    inner = (jax.nn.silu(pair[..., :inner_width]) * pair[..., inner_width:]).astype(BF16)
    result = jnp.einsum("necf,efd->necd", inner, w_expert_out, preferred_element_type=F32).astype(BF16)
    returned = lax.all_to_all(result, ("prompt", "seq"), split_axis=0, concat_axis=0, tiled=True)
    expert_out = lax.dot_general(
        combine,
        returned.reshape(experts_all * CAP, width),
        (((0,), (0,)), ((), ())),
        preferred_element_type=F32,
    ).astype(BF16)
    return (attended[None], expert_out[None], final[None])


def solution(mesh):
    return jax.shard_map(
        shards,
        mesh=mesh,
        in_specs=(
            P("prompt", "seq", None),
            P("prompt"),
            P("prompt"),
            P("prompt", "seq", None),
            P(None, "seq", None, None),
            P(),
            P(None, "seq"),
            P(None, "seq"),
            P(None, "seq"),
            P(None, "seq"),
            P(None, None, "seq"),
            P("seq"),
            P(),
            P("seq", None),
            P(),
            P(),
            P(("prompt", "seq"), None, None),
            P(("prompt", "seq"), None, None),
        ),
        out_specs=(
            P("prompt", "seq", None),
            P("prompt", "seq", None),
            P("prompt", "seq", None, None),
        ),
        check_vma=False,
    )
```

time: 978 us -> 487 us (0.50)
  other arithmetic: 353 us -> 7.39 us
  matrix products: 136 us -> 39 us
  local copies, waits for them, and re-layouts: 106 us -> 22.2 us
  Pallas kernels: 0 us -> 45.4 us
    another operation x11 -> x0, other arithmetic: 323 us -> none  [the longest x4 319 us: block_prepare(): jax.scipy.linalg.solve_triangular(system, right, lower=True, unit_diagona...]
    dot_general x40 -> x4, matrix products: 99.9 us -> 8.49 us  [the longest x1 5.54 us: shards(): lax.dot_general(combine, returned.reshape(experts_all * CAP, width), (((0...]
    pallas_call x0 -> x1, Pallas kernels: none -> 45.4 us  [delta(): pl.pallas_call(functools.partial(delta_kernel, tile), grid=(span // tile,...]
    another operation x16 -> x0, local copies, waits for them, and re-layouts: 16.8 us -> none
    scatter x1 -> x0, local copies, waits for them, and re-layouts: 15.6 us -> none  [shards(): jnp.zeros((experts_all * CAP, width), jnp.bfloat16).at[target].set(sources)]
    gather x1 -> x0, local copies, waits for them, and re-layouts: 15.3 us -> none  [shards(): returned.reshape(experts_all * CAP, width)[target]]
    reduce_sum x4 -> x1, other arithmetic: 11.4 us -> 0.06 us  [shards(): weights = powers / jnp.sum(powers, axis=-1, keepdims=True) * own_live]
    convert_element_type x2 -> x1, local copies, waits for them, and re-layouts: 21.6 us -> 11.2 us  [shards(): jnp.einsum('necf,efd->necd', inner, w_expert_out, preferred_element_type=...]
  transfers between devices with their start and end apart: 3 -> 3, of which waited for: 3 -> 3; matrix products, arithmetic and copies ran while one was open for 1% -> 2% of each run, Pallas kernels for 0% -> 0%
where the time goes in v1:
time: 487 us; the launch traced here: 486 us
  waiting for transfers between devices  245 us (50%)
  blocking collectives  106 us (22%)
  Pallas kernels  45.4 us (9%)
  matrix products  39 us (8%)
  local copies, waits for them, and re-layouts  22.2 us (5%)
  between operations  15.6 us (3%)
  other arithmetic  7.39 us (2%)
  starting transfers between devices  6.06 us (1%)
    all_to_all x1, blocking collectives, shards(): lax.all_to_all(outgoing.reshape(owners, local_experts, CAP, width), ('pro...  106 us
    all_to_all x1, waiting for transfers between devices, shards(): lax.all_to_all(result, ('prompt', 'seq'), split_axis=0, concat_axis=0, ti...  101 us
    reduce_scatter x1, waiting for transfers between devices, shards(): lax.psum_scatter(partial, 'seq', scatter_dimension=0, tiled=True)  82.2 us
    all_gather x1, waiting for transfers between devices, shards(): piece = lax.all_gather(normed, 'seq', axis=0, tiled=True)  61.7 us
    pallas_call x1, Pallas kernels, delta(): pl.pallas_call(functools.partial(delta_kernel, tile), grid=(span // tile,...  45.4 us
    dot_general x1, matrix products, shards(): jnp.einsum('necd,edf->necf', arrived, w_expert_in, preferred_element_type...  18.1 us
    dot_general x1, matrix products, shards(): jnp.einsum('necf,efd->necd', inner, w_expert_out, preferred_element_type=...  12.4 us
    convert_element_type x1, local copies, waits for them, and re-layouts, shards(): jnp.einsum('necf,efd->necd', inner, w_expert_out, preferred_element_type=...  11.2 us
  transfers between devices with their start and end apart: 3, of which 3 were waited for; matrix products, arithmetic and copies ran while one was open for 2% of the time, Pallas kernels for 0%

profile of v1, /device:TPU:5, one launch (start us, length us, event | category | flops | bytes accessed | tf_op | source)
XLA Modules:
  0.0 486.2 jit_solution(9404881921245747173)
XLA Ops:
  7.2 1.4 fusion.14
  8.6 2.0 fusion.16
  12.1 0.7 reshape.97
  13.2 0.7 pad_bitcast_fusion.rate_ref
  14.0 0.9 dynamic-slice_bitcast_fusion.first_ref
  14.9 1.9 constant_dynamic-update-slice_fusion.3
  16.8 0.9 constant_dynamic-update-slice_fusion.2
  17.7 2.3 constant_dynamic-update-slice_fusion.1
  20.0 1.1 constant_dynamic-update-slice_fusion
  21.1 1.0 pad_dynamic-update-slice_fusion.w_ref
  22.1 61.7 %all-gather.2.cloned.1.call-done.piece_ref = bf16[2048,2048]{1,0:T(8,128)(2,1)} async-done(((bf16[128,2048]{1,0:T(8,128)(2,1)}), bf16[2048,2048]{1,0:T(8,128)(2,1)}) %all-gather.2.cloned.1.call-update) | async-done | bytes 8388624 | tf_op jit(solution)/shard_map/all_gather | solution.py:207
  83.7 45.4 %shard_map.193 = (bf16[2048,2048]{1,0:T(8,128)(2,1)}, f32[2,128,128]{2,1,0:T(8,128)}) custom-call(s32[1]{0:T(128)} %copy.60.length_ref, bf16[2048,2048]{1,0:T(8,128)(2,1)} %all-gather.2.cloned.1.call-done.piece_ref, bf16[2048,896]{1,0:T(8,128)(2,1)} %pad_dynamic-update-slice_fusion.w_ref, f32[1,128]{1,0:T(1,128)S(1)} %pad_bitcast_fusion.rate_ref, ...), custom_call_target="tpu_custom_call" | custom-call | tf_op jit(solution)/shard_map/pallas_call | solution.py:137
  129.2 0.6 copy-done.7
  130.6 82.2 %reduce-scatter.2.cloned.1.call-done = bf16[128,2048]{1,0:T(8,128)(2,1)} async-done(((bf16[2048,2048]{1,0:T(8,128)(2,1)}), bf16[128,2048]{1,0:T(8,128)(2,1)}) %reduce-scatter.2.cloned.1.call-update) | async-done | bytes 524304 | tf_op jit(solution)/shard_map/reduce_scatter | solution.py:211
  212.8 1.4 multiply_reduce_fusion
  214.2 2.2 multiply_convert_fusion
  216.4 2.4 convolution_convert_fusion
  218.8 105.5 %all_to_all.10 = bf16[128,2,8,2048]{3,2,1,0:T(8,128)(2,1)S(1)} all-to-all(bf16[128,2,8,2048]{3,2,1,0:T(8,128)(2,1)S(1)} %bitcast.65), channel_id=1, replica_groups=mesh['prompt'=8,'seq'=16] {'prompt','seq'}, dimensions={0} | all-to-all | bytes 16777216 | tf_op jit(solution)/shard_map/all_to_all | solution.py:228
  324.3 18.1 %fusion.5 = f32[128,2,8,1024]{3,0,2,1:T(8,128)} fusion(bf16[2,2048,1024]{2,1,0:T(8,128)(2,1)} %param.34, bf16[128,2,8,2048]{3,2,1,0:T(8,128)(2,1)S(1)} %all_to_all.10), kind=kOutput, calls=%fused_computation.8 | convolution fusion | flops 8589934592 | bytes 25165824 | tf_op jit(solution)/shard_map/necd,edf->necf/dot_general | solution.py:235
  342.4 12.4 %convert_bitcast_fusion = bf16[128,2,8,2048]{3,0,2,1:T(8,128)(2,1)} fusion(bf16[2,512,2048]{2,1,0:T(8,128)(2,1)} %param.35, f32[128,2,8,1024]{3,0,2,1:T(8,128)} %fusion.5), kind=kOutput, calls=%fused_computation.3 | convolution fusion | flops 4305453056 | bytes 20971520 | tf_op jit(solution)/shard_map/necf,efd->necd/dot_general | solution.py:238
  354.8 11.2 %copy.43 = bf16[128,2,8,2048]{3,2,1,0:T(8,128)(2,1)} copy(bf16[128,2,8,2048]{3,0,2,1:T(8,128)(2,1)} %convert_bitcast_fusion) | data formatting | bytes 16777216 | tf_op jit(solution)/shard_map/convert_element_type | solution.py:238
  366.0 6.0 %all-to-all-start.1 = ((bf16[128,2,8,2048]{3,2,1,0:T(8,128)(2,1)}), bf16[128,2,8,2048]{3,2,1,0:T(8,128)(2,1)}, u32[]{:S(2)}, u32[]{:S(2)}) async-start(bf16[128,2,8,2048]{3,2,1,0:T(8,128)(2,1)} %copy.43), calls=%async_computation.2 | async-start | bytes 16777216 | tf_op jit(solution)/shard_map/all_to_all | solution.py:239
  372.7 101.2 %all-to-all-done.1 = bf16[128,2,8,2048]{3,2,1,0:T(8,128)(2,1)} async-done(((bf16[128,2,8,2048]{3,2,1,0:T(8,128)(2,1)}), bf16[128,2,8,2048]{3,2,1,0:T(8,128)(2,1)}, u32[]{:S(2)}, u32[]{:S(2)}) %all-to-all-start.1) | async-done | bytes 8388640 | tf_op jit(solution)/shard_map/all_to_all | solution.py:239
  473.8 5.5 %fusion.10 = bf16[1,128,2048]{2,1,0:T(8,128)(2,1)} fusion(bf16[2048,2048]{1,0:T(8,128)(2,1)} %bitcast.19, bf16[256,128]{1,0:T(8,128)(2,1)S(1)} %fusion.26, f32[256,128]{1,0:T(8,128)S(1)} %convolution_select_fusion, f32[8]{0:T(128)S(1)} %iota_convert_fusion), kind=kOutput, calls=%fused_computation.10 | convolution fusion | flops 1074528256 | bytes 9109536 | tf_op jit(solution)/shard_map/dot_general | solution.py:240
  (34 shorter events, 1.8 us)
Async XLA Ops:
  7.2 364.9 %copy-start = (bf16[2048,256]{1,0:T(8,128)(2,1)S(1)}, bf16[2048,256]{1,0:T(8,128)(2,1)}, u32[]{:S(2)}) copy-start(bf16[2048,256]{1,0:T(8,128)(2,1)} %param.33) | copy-start | bytes 3145732
  7.2 9.6 %copy-start.5 = (bf16[2048,128]{1,0:T(8,128)(2,1)S(1)}, bf16[2048,128]{1,0:T(8,128)(2,1)}, u32[]{:S(2)}) copy-start(bf16[2048,128]{1,0:T(8,128)(2,1)} %param.25) | copy-start | bytes 1572868
  7.2 76.5 %all-gather.2.cloned.1.call-start = ((), (), s32[]{:S(2)}) async-start(), calls=%async_computation.3 | async-start | bytes 8912896 | tf_op jit(solution)/shard_map/all_gather | solution.py:207
  10.7 73.1 %copy-start.1 = (bf16[256,2048]{1,0:T(8,128)(2,1)S(1)}, bf16[256,2048]{1,0:T(8,128)(2,1)}, u32[]{:S(2)}) copy-start(bf16[256,2048]{1,0:T(8,128)(2,1)} %wo_ref.1) | copy-start | bytes 3145732
  10.7 73.1 %copy-start.2 = (f32[128]{0:T(128)S(1)}, f32[128]{0:T(128)}, u32[]{:S(2)}) copy-start(f32[128]{0:T(128)} %param.30) | copy-start | bytes 1540
  10.7 202.1 %reduce-scatter.2.cloned.1.call-start = ((), (), s32[]{:S(2)}) async-start(), calls=%async_computation.4 | async-start | bytes 8912896 | tf_op jit(solution)/shard_map/reduce_scatter | solution.py:211
  13.2 6.8 %copy-start.4 = (bf16[2048,256]{1,0:T(8,128)(2,1)S(1)}, bf16[2048,256]{1,0:T(8,128)(2,1)}, u32[]{:S(2)}) copy-start(bf16[2048,256]{1,0:T(8,128)(2,1)} %param.27) | copy-start | bytes 3145732
  129.2 0.7 copy-start.7
  129.2 83.6 %copy-start.3 = (bf16[1,128,2048]{2,1,0:T(8,128)(2,1)S(1)}, bf16[1,128,2048]{2,1,0:T(8,128)(2,1)}, u32[]{:S(2)}) copy-start(bf16[1,128,2048]{2,1,0:T(8,128)(2,1)} %param.18) | copy-start | bytes 1572868
  129.2 85.0 %copy-start.6 = (f32[2048]{0:T(1024)S(1)}, f32[2048]{0:T(1024)}, u32[]{:S(2)}) copy-start(f32[2048]{0:T(1024)} %param.32) | copy-start | bytes 24580
  366.0 107.8 %all-to-all-start.1 = ((bf16[128,2,8,2048]{3,2,1,0:T(8,128)(2,1)}), bf16[128,2,8,2048]{3,2,1,0:T(8,128)(2,1)}, u32[]{:S(2)}, u32[]{:S(2)}) async-start(bf16[128,2,8,2048]{3,2,1,0:T(8,128)(2,1)} %copy.43), calls=%async_computation.2 | async-start | bytes 16777216 | tf_op jit(solution)/shard_map/all_to_all | solution.py:239
Sparse Core Ops, SparseCore 0:
  10.8 72.9 all-gather.1
  129.3 83.4 reduce-scatter.1
